TPU v7x, 32 devices: a whole 2x2x4 slice. The times are simulated.
32 devices in a mesh: expert: 16 (over z, y, core), dp: 2 (over x).
Axes of the slice: x: 2, y: 2, z: 4, core: 2. Of those that a mesh axis runs over, the one named last changes fastest.
Arguments:
- tokens: bfloat16 [256, 196, 384], P(('expert', 'dp')), may hold values from -6 to 6
- router: bfloat16 [384, 32], replicated, may hold values from -1 to 65
- expert_in: bfloat16 [32, 384, 1536], P('expert'), may hold values from -2.5 to 2.5
- expert_out: bfloat16 [32, 1536, 384], P('expert'), may hold values from -0.15625 to 0.15625
- out_grad: bfloat16 [256, 196, 384], P(('expert', 'dp')), may hold values from -6 to 6
Outputs:
- grad_tokens: bfloat16 [256, 196, 384], P(('expert', 'dp'))
- grad_in: float32 [32, 384, 1536], P('expert', None, 'dp')
- grad_out: float32 [32, 1536, 384], P('expert', 'dp')
- grad_router: float32 [384, 32], replicated
All inputs are finite; a program needn't handle non-finite values.
Results may differ from a plain program's by a relative error of at most 0.017.
Values may be sent and summed in bfloat16 or wider, within the bound.
A program may use at most 64 MiB of HBM per device.

v0:
```python
import jax
import jax.numpy as jnp
from jax import lax
from jax.sharding import PartitionSpec as P


def on_device(tokens, router, expert_in, expert_out, out_grad):
    logits = jnp.einsum("bpd,ds->bps", tokens, router, preferred_element_type=jnp.float32)
    dispatch = jax.nn.softmax(logits, axis=1)
    combine = jax.nn.softmax(logits, axis=2)
    dispatch_low = dispatch.astype(jnp.bfloat16)
    combine_low = combine.astype(jnp.bfloat16)
    slots = jnp.einsum(
        "bps,bpd->bsd", dispatch_low, tokens, preferred_element_type=jnp.float32
    ).astype(jnp.bfloat16)
    slot_grads = jnp.einsum(
        "bps,bpd->bsd", combine_low, out_grad, preferred_element_type=jnp.float32
    ).astype(jnp.bfloat16)
    slots_here, grads_here = (
        lax.all_to_all(slots, "expert", split_axis=1, concat_axis=0, tiled=True),
        lax.all_to_all(slot_grads, "expert", split_axis=1, concat_axis=0, tiled=True),
    )
    hidden = jnp.einsum("rjd,jdf->rjf", slots_here, expert_in, preferred_element_type=jnp.float32)
    activated, gelu_back = jax.vjp(jax.nn.gelu, hidden)
    activated_low = activated.astype(jnp.bfloat16)
    outputs_here = jnp.einsum(
        "rjf,jfd->rjd", activated_low, expert_out, preferred_element_type=jnp.float32
    ).astype(jnp.bfloat16)
    act_grad = jnp.einsum(
        "rjd,jfd->rjf", grads_here, expert_out, preferred_element_type=jnp.float32
    )
    hidden_grad = gelu_back(act_grad)[0].astype(jnp.bfloat16)
    input_grad_here = jnp.einsum(
        "rjf,jdf->rjd", hidden_grad, expert_in, preferred_element_type=jnp.float32
    ).astype(jnp.bfloat16)
    outputs, inputs_grad = (
        lax.all_to_all(outputs_here, "expert", split_axis=0, concat_axis=1, tiled=True),
        lax.all_to_all(input_grad_here, "expert", split_axis=0, concat_axis=1, tiled=True),
    )
    first_term = jnp.einsum(
        "rjd,rjf->jdf", slots_here, hidden_grad, preferred_element_type=jnp.float32
    )
    second_term = jnp.einsum(
        "rjf,rjd->jfd", activated_low, grads_here, preferred_element_type=jnp.float32
    )
    grad_in = lax.psum_scatter(
        first_term.astype(jnp.bfloat16), "dp", scatter_dimension=2, tiled=True
    ).astype(jnp.float32)
    grad_out = lax.psum_scatter(
        second_term.astype(jnp.bfloat16), "dp", scatter_dimension=1, tiled=True
    ).astype(jnp.float32)
    combine_grad = jnp.einsum("bpd,bsd->bps", out_grad, outputs, preferred_element_type=jnp.float32)
    dispatch_grad = jnp.einsum(
        "bpd,bsd->bps", tokens, inputs_grad, preferred_element_type=jnp.float32
    )
    logit_grad = dispatch * (
        dispatch_grad - jnp.sum(dispatch * dispatch_grad, axis=1, keepdims=True)
    )
    logit_grad = logit_grad + combine * (
        combine_grad - jnp.sum(combine * combine_grad, axis=2, keepdims=True)
    )
    logit_low = logit_grad.astype(jnp.bfloat16)
    first_part = jnp.einsum(
        "bps,bsd->bpd", dispatch_low, inputs_grad, preferred_element_type=jnp.float32
    )
    second_part = jnp.einsum("bps,ds->bpd", logit_low, router, preferred_element_type=jnp.float32)
    grad_tokens = (first_part + second_part).astype(jnp.bfloat16)
    router_term = jnp.einsum("bpd,bps->ds", tokens, logit_low, preferred_element_type=jnp.float32)
    grad_router = lax.psum(router_term, ("expert", "dp"))
    return (grad_tokens, grad_in, grad_out, grad_router)


def solution(mesh):
    placed = (
        P(("expert", "dp"), None, None),
        P(),
        P("expert", None, None),
        P("expert", None, None),
        P(("expert", "dp"), None, None),
    )
    return jax.shard_map(
        on_device,
        mesh=mesh,
        in_specs=placed,
        out_specs=(
            P(("expert", "dp"), None, None),
            P("expert", None, "dp"),
            P("expert", "dp", None),
            P(),
        ),
        check_vma=False,
    )
```

profile of v0, /device:TPU:0, one launch (start us, length us, event | category | flops | bytes accessed | tf_op | source)
XLA Modules:
  0.0 145.3 jit_solution(13470126646856257983)
XLA Ops:
  7.2 0.0 copy-start
  7.2 2.0 %fusion.56 = (f32[8,196]{0,1:T(8,128)S(1)}, f32[8,32]{1,0:T(8,128)S(1)}, f32[8,196,32]{2,0,1:T(8,128)S(1)}) fusion(bf16[8,196,384]{2,0,1:T(8,128)(2,1)} %param.5, bf16[384,32]{0,1:T(8,128)(2,1)} %param.6), kind=kOutput, calls=%fused_computation.67 | convolution fusion | flops 38633696 | bytes 1436800 | tf_op jit(solution)/shard_map/bpd,ds->bps/dot_general | solution.py:8
  9.2 0.3 copy.40
  9.5 0.1 copy.44
  9.6 0.2 fusion.30
  9.8 1.8 %convolution_convert_fusion.2 = bf16[8,32,384]{2,1,0:T(8,128)(2,1)S(1)} fusion(bf16[8,196,384]{2,0,1:T(8,128)(2,1)} %param.5, f32[8,196,32]{1,2,0:T(8,128)S(1)} %copy.40, f32[8,32]{1,0:T(8,128)S(1)} %get-tuple-element.15, f32[8,32]{1,0:T(8,128)S(1)} %get-tuple-element.13), kind=kOutput, calls=%fused_computation.17 | convolution fusion | flops 38784000 | bytes 1603584 | tf_op jit(solution)/shard_map/bps,bpd->bsd/dot_general | solution.py:13
  11.6 0.8 copy.27
  12.4 7.4 %all-to-all-start.1 = ((bf16[8,32,384]{2,0,1:T(8,128)(2,1)}), bf16[8,32,384]{2,0,1:T(8,128)(2,1)S(1)}, u32[]{:S(2)}, u32[]{:S(2)}) async-start(bf16[8,32,384]{2,0,1:T(8,128)(2,1)} %copy.27), calls=%async_computation.1 | async-start | bytes 393216 | tf_op jit(solution)/shard_map/all_to_all | solution.py:20
  19.8 1.7 %convolution_convert_fusion.3 = bf16[8,32,384]{2,1,0:T(8,128)(2,1)S(1)} fusion(bf16[8,196,384]{2,0,1:T(8,128)(2,1)} %param.9, f32[8,196,32]{1,2,0:T(8,128)S(1)} %copy.40, f32[8,196]{1,0:T(8,128)S(1)} %get-tuple-element.14, f32[8,196]{1,0:T(8,128)S(1)} %copy.44), kind=kOutput, calls=%fused_computation.18 | convolution fusion | flops 38784000 | bytes 1614080 | tf_op jit(solution)/shard_map/bps,bpd->bsd/dot_general | solution.py:16
  21.5 0.8 copy.24
  22.3 6.5 %all-to-all-done.1 = bf16[8,32,384]{2,0,1:T(8,128)(2,1)S(1)} async-done(((bf16[8,32,384]{2,0,1:T(8,128)(2,1)}), bf16[8,32,384]{2,0,1:T(8,128)(2,1)S(1)}, u32[]{:S(2)}, u32[]{:S(2)}) %all-to-all-start.1) | async-done | bytes 196640 | tf_op jit(solution)/shard_map/all_to_all | solution.py:20
  28.8 3.5 %all-to-all-start = ((bf16[8,32,384]{2,0,1:T(8,128)(2,1)}), bf16[8,32,384]{2,0,1:T(8,128)(2,1)S(1)}, u32[]{:S(2)}, u32[]{:S(2)}) async-start(bf16[8,32,384]{2,0,1:T(8,128)(2,1)} %copy.24), calls=%async_computation | async-start | bytes 393216 | tf_op jit(solution)/shard_map/all_to_all | solution.py:21
  32.3 0.0 reduce-scatter.5.cloned.1.call-start
  32.3 3.4 %convolution_bitcast_fusion = f32[128,2,1536]{2,0,1:T(8,128)} fusion(bf16[2,384,1536]{2,1,0:T(8,128)(2,1)} %param.7, bf16[8,16,2,384]{3,0,2,1:T(8,128)(2,1)S(1)} %bitcast.59), kind=kOutput, calls=%fused_computation.4 | convolution fusion | flops 301989888 | bytes 4128768 | tf_op jit(solution)/shard_map/rjd,jdf->rjf/dot_general | solution.py:23
  35.7 0.0 copy-done.2
  35.7 5.5 %all-to-all-done = bf16[8,32,384]{2,0,1:T(8,128)(2,1)S(1)} async-done(((bf16[8,32,384]{2,0,1:T(8,128)(2,1)}), bf16[8,32,384]{2,0,1:T(8,128)(2,1)S(1)}, u32[]{:S(2)}, u32[]{:S(2)}) %all-to-all-start) | async-done | bytes 196640 | tf_op jit(solution)/shard_map/all_to_all | solution.py:21
  41.3 3.7 %convolution_convert_fusion = bf16[2,1536,384]{2,1,0:T(8,128)(2,1)} fusion(bf16[8,16,2,384]{3,0,2,1:T(8,128)(2,1)S(1)} %bitcast.64, f32[128,2,1536]{2,0,1:T(8,128)} %convolution_bitcast_fusion), kind=kOutput, calls=%fused_computation.2 | convolution fusion | flops 306708480 | bytes 4128768 | tf_op jit(solution)/shard_map/rjf,rjd->jfd/dot_general | solution.py:43
  45.0 0.0 copy-done.4
  45.0 0.0 reduce-scatter.5.cloned.1.call-update
  45.0 0.0 reduce-scatter.3.cloned.1.call-start
  45.1 0.0 copy-done
  45.1 0.0 copy-start.3
  45.1 2.9 %fusion.8 = bf16[128,2,1536]{2,0,1:T(8,128)(2,1)S(1)} fusion(f32[128,2,1536]{2,0,1:T(8,128)} %convolution_bitcast_fusion, bf16[2,1536,384]{2,1,0:T(8,128)(2,1)S(1)} %copy-done, bf16[8,16,2,384]{3,0,2,1:T(8,128)(2,1)} %bitcast.65), kind=kOutput, calls=%fused_computation.15 | convolution fusion | flops 309854208 | bytes 4915200 | tf_op jit(solution)/shard_map/rjd,jfd->rjf/dot_general | solution.py:29
  48.0 2.2 %convolution_convert_fusion.1 = bf16[2,384,1536]{2,1,0:T(8,128)(2,1)} fusion(bf16[128,2,1536]{2,0,1:T(8,128)(2,1)S(1)} %fusion.8, bf16[8,16,2,384]{3,0,2,1:T(8,128)(2,1)S(1)} %bitcast.60), kind=kOutput, calls=%fused_computation.3 | convolution fusion | flops 303169536 | bytes 3342336 | tf_op jit(solution)/shard_map/rjd,rjf->jdf/dot_general | solution.py:40
  50.2 0.0 reduce-scatter.3.cloned.1.call-update
  50.3 2.1 %fusion.16 = bf16[128,2,384]{2,0,1:T(8,128)(2,1)S(1)} fusion(bf16[2,1536,384]{2,1,0:T(8,128)(2,1)S(1)} %copy-done, f32[128,2,1536]{2,0,1:T(8,128)} %convolution_bitcast_fusion), kind=kOutput, calls=%fused_computation.30 | convolution fusion | flops 305627136 | bytes 4128768 | tf_op jit(solution)/shard_map/rjf,jfd->rjd/dot_general | solution.py:26
  52.4 0.9 copy.32
  53.3 4.2 %all-to-all-start.3 = ((bf16[128,2,384]{2,1,0:T(2,128)(2,1)}), bf16[128,2,384]{2,1,0:T(2,128)(2,1)}, u32[]{:S(2)}, u32[]{:S(2)}) async-start(bf16[128,2,384]{2,1,0:T(2,128)(2,1)} %copy.32), calls=%async_computation.3 | async-start | bytes 393216 | tf_op jit(solution)/shard_map/all_to_all | solution.py:37
  57.5 2.5 %fusion.15 = bf16[128,2,384]{2,0,1:T(8,128)(2,1)S(1)} fusion(bf16[128,2,1536]{2,0,1:T(8,128)(2,1)S(1)} %fusion.8, bf16[2,384,1536]{2,1,0:T(8,128)(2,1)} %param.7), kind=kOutput, calls=%fused_computation.29 | convolution fusion | flops 302088192 | bytes 3342336 | tf_op jit(solution)/shard_map/rjf,jdf->rjd/dot_general | solution.py:33
  60.0 0.9 copy.29
  60.9 5.6 %all-to-all-done.3 = bf16[128,2,384]{2,1,0:T(2,128)(2,1)} async-done(((bf16[128,2,384]{2,1,0:T(2,128)(2,1)}), bf16[128,2,384]{2,1,0:T(2,128)(2,1)}, u32[]{:S(2)}, u32[]{:S(2)}) %all-to-all-start.3) | async-done | bytes 196640 | tf_op jit(solution)/shard_map/all_to_all | solution.py:37
  66.5 3.5 %all-to-all-start.2 = ((bf16[128,2,384]{2,1,0:T(2,128)(2,1)}), bf16[128,2,384]{2,1,0:T(2,128)(2,1)S(1)}, u32[]{:S(2)}, u32[]{:S(2)}) async-start(bf16[128,2,384]{2,1,0:T(2,128)(2,1)} %copy.29), calls=%async_computation.2 | async-start | bytes 393216 | tf_op jit(solution)/shard_map/all_to_all | solution.py:38
  70.0 1.1 copy.73
  71.1 0.1 all_to_all.67
  71.2 7.8 %all-to-all-done.2 = bf16[128,2,384]{2,1,0:T(2,128)(2,1)S(1)} async-done(((bf16[128,2,384]{2,1,0:T(2,128)(2,1)}), bf16[128,2,384]{2,1,0:T(2,128)(2,1)S(1)}, u32[]{:S(2)}, u32[]{:S(2)}) %all-to-all-start.2) | async-done | bytes 196640 | tf_op jit(solution)/shard_map/all_to_all | solution.py:38
  79.0 0.1 copy.74
  79.1 0.1 all_to_all.63
  79.2 0.0 copy-start.1
  79.2 2.0 %convolution_bitcast_fusion.2 = f32[8,196,32]{1,2,0:T(8,128)S(1)} fusion(bf16[8,32,384]{2,1,0:T(8,128)(2,1)S(1)} %all_to_all.67, bf16[8,196,384]{2,0,1:T(8,128)(2,1)} %param.9), kind=kOutput, calls=%fused_computation.26 | convolution fusion | flops 38535168 | bytes 1601536 | tf_op jit(solution)/shard_map/bpd,bsd->bps/dot_general | solution.py:52
  81.2 0.6 fusion.13
  81.8 0.6 convolution_bitcast_fusion.3
  82.4 2.5 %fusion.40 = f32[8,196,384]{2,1,0:T(8,128)} fusion(bf16[8,32,384]{2,1,0:T(8,128)(2,1)S(1)} %all_to_all.63, f32[8,196,32]{1,2,0:T(8,128)S(1)} %copy.40, f32[8,32]{1,0:T(8,128)S(1)} %get-tuple-element.15, f32[8,32]{1,0:T(8,128)S(1)} %get-tuple-element.13), kind=kOutput, calls=%fused_computation.59 | convolution fusion | flops 38685696 | bytes 2807808 | tf_op jit(solution)/shard_map/bps,bsd->bpd/dot_general | solution.py:63
  84.9 3.9 %add_convert_fusion = bf16[8,196,384]{2,1,0:T(8,128)(2,1)} fusion(f32[8,196,384]{2,1,0:T(8,128)} %fusion.40, f32[8,196,32]{1,2,0:T(8,128)S(1)} %fusion.13, f32[8,196,32]{1,2,0:T(8,128)S(1)} %convolution_bitcast_fusion.3, bf16[384,32]{0,1:T(8,128)(2,1)S(1)} %copy-done.5, f32[8,196,32]{1,2,0:T(8,128)S(1)} %copy.40, f32[8,32]{1,0:T(8,128)S(1)} %get-tuple-element.15, ...), kind=kOutput, calls=%fused_computation.6 | convolution fusion | flops 40191428 | bytes 4241408 | tf_op jit(solution)/shard_map/bps,ds->bpd/dot_general | solution.py:66
  88.8 2.5 %copy.38 = bf16[8,196,384]{2,0,1:T(8,128)(2,1)} copy(bf16[8,196,384]{2,1,0:T(8,128)(2,1)} %add_convert_fusion) | data formatting | bytes 2408448
  91.2 2.4 %convolution_bitcast_fusion.4 = f32[384,32]{0,1:T(8,128)S(1)} fusion(f32[8,196,32]{1,2,0:T(8,128)S(1)} %fusion.13, f32[8,196,32]{1,2,0:T(8,128)S(1)} %convolution_bitcast_fusion.3, bf16[8,196,384]{2,0,1:T(8,128)(2,1)} %param.5, f32[8,196,32]{1,2,0:T(8,128)S(1)} %copy.40, f32[8,32]{1,0:T(8,128)S(1)} %get-tuple-element.15, f32[8,32]{1,0:T(8,128)S(1)} %get-tuple-element.13), kind=kOutput, calls=%fused_computation.31 | convolution fusion | flops 38987204 | bytes 1857536 | tf_op jit(solution)/shard_map/bpd,bps->ds/dot_general | solution.py:68
  93.6 39.2 %psum.7 = f32[384,32]{0,1:T(8,128)} all-reduce(f32[384,32]{0,1:T(8,128)S(1)} %convolution_bitcast_fusion.4), channel_id=1, replica_groups=mesh['expert'=16,'dp'=2] {'expert','dp'}, use_global_device_ids=true, to_apply=%region_8.0 | all-reduce | flops 12288 | bytes 98304 | tf_op jit(solution)/shard_map/psum | solution.py:69
  132.8 2.8 %convert_element_type.63 = f32[2,768,384]{2,1,0:T(8,128)} convert(bf16[2,768,384]{2,1,0:T(8,128)(2,1)} %reduce-scatter.5.cloned.1.call-done) | non-fusion elementwise | flops 589824 | bytes 3538944 | tf_op jit(solution)/shard_map/convert_element_type | solution.py:51
  135.7 2.8 %convert_element_type.61 = f32[2,384,768]{2,1,0:T(8,128)} convert(bf16[2,384,768]{2,1,0:T(8,128)(2,1)} %reduce-scatter.3.cloned.1.call-done) | non-fusion elementwise | flops 589824 | bytes 3538944 | tf_op jit(solution)/shard_map/convert_element_type | solution.py:48
  (8 shorter events, 0.0 us)
Async XLA Ops:
  7.2 37.9 %copy-start = (bf16[2,1536,384]{2,1,0:T(8,128)(2,1)S(1)}, bf16[2,1536,384]{2,1,0:T(8,128)(2,1)}, u32[]{:S(2)}) copy-start(bf16[2,1536,384]{2,1,0:T(8,128)(2,1)} %param.8) | copy-start | bytes 7077892
  12.4 16.4 %all-to-all-start.1 = ((bf16[8,32,384]{2,0,1:T(8,128)(2,1)}), bf16[8,32,384]{2,0,1:T(8,128)(2,1)S(1)}, u32[]{:S(2)}, u32[]{:S(2)}) async-start(bf16[8,32,384]{2,0,1:T(8,128)(2,1)} %copy.27), calls=%async_computation.1 | async-start | bytes 393216 | tf_op jit(solution)/shard_map/all_to_all | solution.py:20
  28.8 7.0 %copy-start.2 = (bf16[8,32,384]{2,0,1:T(8,128)(2,1)}, bf16[8,32,384]{2,0,1:T(8,128)(2,1)S(1)}, u32[]{:S(2)}) copy-start(bf16[8,32,384]{2,0,1:T(8,128)(2,1)S(1)} %all-to-all-done.1) | copy-start | bytes 589828
  28.8 12.5 %all-to-all-start = ((bf16[8,32,384]{2,0,1:T(8,128)(2,1)}), bf16[8,32,384]{2,0,1:T(8,128)(2,1)S(1)}, u32[]{:S(2)}, u32[]{:S(2)}) async-start(bf16[8,32,384]{2,0,1:T(8,128)(2,1)} %copy.24), calls=%async_computation | async-start | bytes 393216 | tf_op jit(solution)/shard_map/all_to_all | solution.py:21
  32.3 100.5 %reduce-scatter.5.cloned.1.call-start = ((), (), s32[]{:S(2)}) async-start(), calls=%async_computation.7 | async-start | bytes 3538944 | tf_op jit(solution)/shard_map/reduce_scatter | solution.py:49
  41.2 3.7 %copy-start.4 = (bf16[8,32,384]{2,0,1:T(8,128)(2,1)}, bf16[8,32,384]{2,0,1:T(8,128)(2,1)S(1)}, u32[]{:S(2)}) copy-start(bf16[8,32,384]{2,0,1:T(8,128)(2,1)S(1)} %all-to-all-done) | copy-start | bytes 589828
  45.0 90.6 %reduce-scatter.3.cloned.1.call-start = ((), (), s32[]{:S(2)}) async-start(), calls=%async_computation.6 | async-start | bytes 3538944 | tf_op jit(solution)/shard_map/reduce_scatter | solution.py:46
  45.1 2.9 %copy-start.3 = (bf16[8,32,384]{2,0,1:T(8,128)(2,1)S(1)}, bf16[8,32,384]{2,0,1:T(8,128)(2,1)}, u32[]{:S(2)}) copy-start(bf16[8,32,384]{2,0,1:T(8,128)(2,1)} %copy-done.2) | copy-start | bytes 589828
  53.3 13.2 %all-to-all-start.3 = ((bf16[128,2,384]{2,1,0:T(2,128)(2,1)}), bf16[128,2,384]{2,1,0:T(2,128)(2,1)}, u32[]{:S(2)}, u32[]{:S(2)}) async-start(bf16[128,2,384]{2,1,0:T(2,128)(2,1)} %copy.32), calls=%async_computation.3 | async-start | bytes 393216 | tf_op jit(solution)/shard_map/all_to_all | solution.py:37
  66.5 12.5 %all-to-all-start.2 = ((bf16[128,2,384]{2,1,0:T(2,128)(2,1)}), bf16[128,2,384]{2,1,0:T(2,128)(2,1)S(1)}, u32[]{:S(2)}, u32[]{:S(2)}) async-start(bf16[128,2,384]{2,1,0:T(2,128)(2,1)} %copy.29), calls=%async_computation.2 | async-start | bytes 393216 | tf_op jit(solution)/shard_map/all_to_all | solution.py:38
  79.2 2.6 %copy-start.1 = (bf16[8,196,384]{2,0,1:T(8,128)(2,1)S(1)}, bf16[8,196,384]{2,0,1:T(8,128)(2,1)}, u32[]{:S(2)}) copy-start(bf16[8,196,384]{2,0,1:T(8,128)(2,1)} %param.5) | copy-start | bytes 3612676
  82.4 2.5 %copy-start.5 = (bf16[384,32]{0,1:T(8,128)(2,1)S(1)}, bf16[384,32]{0,1:T(8,128)(2,1)}, u32[]{:S(2)}) copy-start(bf16[384,32]{0,1:T(8,128)(2,1)} %param.6) | copy-start | bytes 73732
Sparse Core Ops, SparseCore 0:
  45.1 32.6 reduce-scatter.4
  80.7 35.4 reduce-scatter.2
where the time goes:
time: 146 us; the launch traced here: 145 us
  blocking collectives  39.2 us (27%)
  matrix products  33.7 us (23%)
  waiting for transfers between devices  25.5 us (17%)
  starting transfers between devices  18.7 us (13%)
  between operations  14.2 us (10%)
  local copies, waits for them, and re-layouts  7.55 us (5%)
  other arithmetic  6.52 us (4%)
    psum x1, blocking collectives, on_device(): grad_router = lax.psum(router_term, ('expert', 'dp'))  39.2 us
    all_to_all x1, waiting for transfers between devices, on_device(): lax.all_to_all(input_grad_here, 'expert', split_axis=0, concat_axis=1, ti...  7.81 us
    all_to_all x1, starting transfers between devices, on_device(): lax.all_to_all(slots, 'expert', split_axis=1, concat_axis=0, tiled=True)  7.39 us
    all_to_all x1, waiting for transfers between devices, on_device(): lax.all_to_all(slots, 'expert', split_axis=1, concat_axis=0, tiled=True)  6.49 us
    all_to_all x1, waiting for transfers between devices, on_device(): lax.all_to_all(outputs_here, 'expert', split_axis=0, concat_axis=1, tiled...  5.62 us
    all_to_all x1, waiting for transfers between devices, on_device(): lax.all_to_all(slot_grads, 'expert', split_axis=1, concat_axis=0, tiled=T...  5.51 us
    all_to_all x1, starting transfers between devices, on_device(): lax.all_to_all(outputs_here, 'expert', split_axis=0, concat_axis=1, tiled...  4.17 us
    dot_general x1, matrix products, on_device(): jnp.einsum('bps,ds->bpd', logit_low, router, preferred_element_type=jnp.f...  3.85 us
  transfers between devices with their start and end apart: 6, of which 4 were waited for; matrix products, arithmetic and copies ran while one was open for 25% of the time, Pallas kernels for 0%

commit v1 on v0

v1 whole, which is shorter than its diff:
```python
import functools

import jax
import jax.numpy as jnp
from jax import lax
from jax.sharding import PartitionSpec as P


def to_experts(x, n):
    wide = lax.all_to_all(x, "expert", split_axis=0, concat_axis=1, tiled=True)
    return wide.reshape(wide.shape[0], n, x.shape[1], x.shape[2])


def to_images(x, n):
    flat = x.reshape(x.shape[0], n * x.shape[2], x.shape[3])
    return lax.all_to_all(flat, "expert", split_axis=1, concat_axis=0, tiled=True)


def sum_all(x, n, dp):
    return lax.psum(x, ("expert", "dp"))


def on_device(n, dp, tokens, router, expert_in, expert_out, out_grad):
    f32, low = jnp.float32, jnp.bfloat16
    dot = functools.partial(jnp.einsum, preferred_element_type=f32)
    images = tokens.shape[0]
    logits = dot("bpd,ds->bps", tokens, router)
    dispatch = jax.nn.softmax(logits, axis=1)
    combine = jax.nn.softmax(logits, axis=2)
    dispatch_low = dispatch.astype(low)
    combine_low = combine.astype(low)
    slots = dot("bps,bpd->sbd", dispatch_low, tokens).astype(low)
    slot_grads = dot("bps,bpd->sbd", combine_low, out_grad).astype(low)
    here = to_experts(jnp.concatenate([slots, slot_grads], axis=1), n)
    each, width = here.shape[0], here.shape[3]
    everyone = lax.all_gather(here, "dp", axis=1, tiled=True)

    def halves(block):
        flat = (each, block.shape[1] * images, width)
        return block[:, :, :images].reshape(flat), block[:, :, images:].reshape(flat)

    def hidden_side(inputs, grads, first, second):
        hidden = dot("jrd,jdf->jrf", inputs, first)
        activated, gelu_back = jax.vjp(jax.nn.gelu, hidden)
        act_grad = dot("jrd,jfd->jrf", grads, second)
        return activated.astype(low), gelu_back(act_grad)[0].astype(low)

    slots_here, grads_here = halves(here)
    activated, hidden_grad = hidden_side(slots_here, grads_here, expert_in, expert_out)
    outputs_here = dot("jrf,jfd->jrd", activated, expert_out).astype(low)
    input_grad_here = dot("jrf,jdf->jrd", hidden_grad, expert_in).astype(low)
    split = (each, n, images, width)
    back = to_images(
        jnp.concatenate([outputs_here.reshape(split), input_grad_here.reshape(split)], axis=2), n
    )
    outputs, inputs_grad = back[:, :images], back[:, images:]

    units = expert_in.shape[2] // dp
    start = lax.axis_index("dp") * units
    first = lax.dynamic_slice_in_dim(expert_in, start, units, axis=2)
    second = lax.dynamic_slice_in_dim(expert_out, start, units, axis=1)
    slots_all, grads_all = halves(everyone)
    activated_all, hidden_grad_all = hidden_side(slots_all, grads_all, first, second)
    grad_in = dot("jrd,jrf->jdf", slots_all, hidden_grad_all)
    grad_out = dot("jrf,jrd->jfd", activated_all, grads_all)

    combine_grad = dot("bpd,sbd->bps", out_grad, outputs)
    dispatch_grad = dot("bpd,sbd->bps", tokens, inputs_grad)
    logit_grad = dispatch * (
        dispatch_grad - jnp.sum(dispatch * dispatch_grad, axis=1, keepdims=True)
    )
    logit_grad = logit_grad + combine * (
        combine_grad - jnp.sum(combine * combine_grad, axis=2, keepdims=True)
    )
    logit_low = logit_grad.astype(low)
    first_part = dot("bps,sbd->bpd", dispatch_low, inputs_grad)
    second_part = dot("bps,ds->bpd", logit_low, router)
    grad_tokens = (first_part + second_part).astype(low)
    router_term = dot("bps,bpd->sd", logit_low, tokens)
    grad_router = sum_all(router_term, n, dp).T
    return (grad_tokens, grad_in, grad_out, grad_router)


def solution(mesh):
    placed = (
        P(("expert", "dp"), None, None),
        P(),
        P("expert", None, None),
        P("expert", None, None),
        P(("expert", "dp"), None, None),
    )
    return jax.shard_map(
        functools.partial(on_device, mesh.shape["expert"], mesh.shape["dp"]),
        mesh=mesh,
        in_specs=placed,
        out_specs=(
            P(("expert", "dp"), None, None),
            P("expert", None, "dp"),
            P("expert", "dp", None),
            P(),
        ),
        check_vma=False,
    )
```

time: 146 us -> 138 us (0.945)
  between operations: 14.2 us -> 0.87 us
  blocking collectives: 39.2 us -> 51.8 us
  waiting for transfers between devices: 25.5 us -> 14.3 us
  other arithmetic: 6.52 us -> 14.9 us
  starting transfers between devices: 18.7 us -> 11.2 us
  local copies, waits for them, and re-layouts: 7.55 us -> 13.9 us
  matrix products: 33.7 us -> 30.8 us
    all_gather x0 -> x1, blocking collectives: none -> 11.9 us  [on_device(): everyone = lax.all_gather(here, 'dp', axis=1, tiled=True)]
    all_to_all x4 -> x2, waiting for transfers between devices: 25.4 us -> 14.3 us  [the longest x1 12.2 us: to_experts(): wide = lax.all_to_all(x, 'expert', split_axis=0, concat_axis=1, tiled=True)]
    sub x1, other arithmetic: 0.64 us -> 10.8 us  [on_device(): combine_grad - jnp.sum(combine * combine_grad, axis=2, keepdims=True)]
    all_to_all x4 -> x2, starting transfers between devices: 18.6 us -> 11.2 us  [the longest x1 7.39 us: to_experts(): wide = lax.all_to_all(x, 'expert', split_axis=0, concat_axis=1, tiled=True)]
    convert_element_type x2, other arithmetic: 5.67 us -> 1.16 us  [the longest x1 0.88 us: on_device(): dispatch_low = dispatch.astype(low)]
    dot_general x1 -> x2, local copies, waits for them, and re-layouts: 0.35 us -> 3.46 us  [the longest x1 2.2 us: on_device(): dispatch_grad = dot('bpd,sbd->bps', tokens, inputs_grad)]
    dot_general x14, matrix products: 33.7 us -> 30.8 us  [the longest x1 5.08 us: on_device(): grad_in = dot('jrd,jrf->jdf', slots_all, hidden_grad_all)]
    unnamed x14 -> x41, local copies, waits for them, and re-layouts: 2.56 us -> 4.81 us
  transfers between devices with their start and end apart: 6 -> 2, of which waited for: 4 -> 2; matrix products, arithmetic and copies ran while one was open for 25% -> 6% of each run, Pallas kernels for 0% -> 0%
where the time goes in v1:
time: 138 us
  blocking collectives  51.8 us (38%)
  matrix products  30.8 us (22%)
  other arithmetic  14.9 us (11%)
  waiting for transfers between devices  14.3 us (10%)
  local copies, waits for them, and re-layouts  13.9 us (10%)
  starting transfers between devices  11.2 us (8%)
    psum x1, blocking collectives, sum_all(): return lax.psum(x, ('expert', 'dp'))  39.9 us
    all_to_all x1, waiting for transfers between devices, to_experts(): wide = lax.all_to_all(x, 'expert', split_axis=0, concat_axis=1, tiled=True)  12.2 us
    all_gather x1, blocking collectives, on_device(): everyone = lax.all_gather(here, 'dp', axis=1, tiled=True)  11.9 us
    sub x1, other arithmetic, on_device(): combine_grad - jnp.sum(combine * combine_grad, axis=2, keepdims=True)  10.8 us
    all_to_all x1, starting transfers between devices, to_experts(): wide = lax.all_to_all(x, 'expert', split_axis=0, concat_axis=1, tiled=True)  7.39 us
    dot_general x1, matrix products, on_device(): grad_in = dot('jrd,jrf->jdf', slots_all, hidden_grad_all)  5.08 us
    unnamed x41, local copies, waits for them, and re-layouts  4.81 us
    dot_general x1, matrix products, on_device(): input_grad_here = dot('jrf,jdf->jrd', hidden_grad, expert_in).astype(low)  4.77 us
  transfers between devices with their start and end apart: 2, of which 2 were waited for; matrix products, arithmetic and copies ran while one was open for 6% of the time, Pallas kernels for 0%

profile of v1, /device:TPU:0, one launch (start us, length us, event | category | flops | bytes accessed | tf_op | source)
XLA Modules:
  0.0 137.6 jit_solution(8672719044527051498)
XLA Ops:
  0.6 0.0 copy-start
  0.6 1.9 %fusion.97 = (f32[8,32]{1,0:T(8,128)S(1)}, f32[8,196,32]{2,0,1:T(8,128)S(1)}) fusion(bf16[8,196,384]{2,0,1:T(8,128)(2,1)} %param.5, bf16[384,32]{0,1:T(8,128)(2,1)} %param.6), kind=kOutput, calls=%fused_computation.114 | convolution fusion | flops 38585088 | bytes 1430528 | tf_op jit(solution)/shard_map/bpd,ds->bps/dot_general | solution.py:27
  2.5 0.0 copy-start.16
  2.5 1.2 fusion.98
  3.7 0.2 fusion.62
  4.0 0.0 copy-start.18
  4.0 0.6 copy-done.18
  4.6 0.9 fusion.96
  5.4 1.2 copy.45
  6.7 0.0 copy-start.2
  6.7 0.0 copy-start.7
  6.7 1.9 %fusion.33 = bf16[32,8,384]{2,0,1:T(8,128)(2,1)S(1)} fusion(bf16[8,196,32]{1,2,0:T(8,128)(2,1)S(1)} %copy.45, bf16[8,196,384]{2,0,1:T(8,128)(2,1)} %param.5), kind=kOutput, calls=%fused_computation.40 | convolution fusion | flops 38633472 | bytes 1501184 | tf_op jit(solution)/shard_map/bps,bpd->sbd/dot_general | solution.py:32
  8.6 0.0 copy-done.12
  8.7 0.3 fusion.95
  9.0 0.5 fusion.34
  9.5 0.0 copy-done.9
  9.5 0.9 copy.40
  10.4 7.4 %all-to-all-start = ((bf16[32,16,384]{2,1,0:T(8,128)(2,1)}), bf16[32,16,384]{2,1,0:T(8,128)(2,1)S(1)}, u32[]{:S(2)}, u32[]{:S(2)}) async-start(bf16[32,16,384]{2,1,0:T(8,128)(2,1)} %copy.40), calls=%async_computation | async-start | bytes 786432 | tf_op jit(solution)/shard_map/all_to_all | solution.py:10
  17.8 12.2 %all-to-all-done = bf16[32,16,384]{2,1,0:T(8,128)(2,1)S(1)} async-done(((bf16[32,16,384]{2,1,0:T(8,128)(2,1)}), bf16[32,16,384]{2,1,0:T(8,128)(2,1)S(1)}, u32[]{:S(2)}, u32[]{:S(2)}) %all-to-all-start) | async-done | bytes 393248 | tf_op jit(solution)/shard_map/all_to_all | solution.py:10
  30.0 0.7 copy-done.5
  30.8 1.0 copy.73
  31.8 11.9 %all_gather.3 = bf16[2,32,16,384]{3,2,1,0:T(8,128)(2,1)} all-gather(bf16[2,16,16,384]{3,2,1,0:T(8,128)(2,1)S(1)} %bitcast.75), channel_id=1, replica_groups=mesh['expert'=16,'dp'=2] {'dp'}, dimensions={1}, use_global_device_ids=true | all-gather | bytes 1179648 | tf_op jit(solution)/shard_map/all_gather | solution.py:36
  43.7 0.0 copy-done
  43.7 1.7 %fusion.68 = f32[2,128,1536]{2,1,0:T(8,128)} fusion(bf16[2,384,1536]{2,1,0:T(8,128)(2,1)S(1)} %copy-done, bf16[2,16,16,384]{3,2,1,0:T(8,128)(2,1)S(1)} %bitcast.76), kind=kOutput, calls=%fused_computation.86 | convolution fusion | flops 301989888 | bytes 4128768 | tf_op jit(solution)/shard_map/jrd,jdf->jrf/dot_general | solution.py:43
  45.4 4.8 %fusion.32 = bf16[2,16,8,384]{3,2,1,0:T(8,128)(2,1)} fusion(bf16[2,384,1536]{2,1,0:T(8,128)(2,1)S(1)} %copy-done, f32[2,128,1536]{2,1,0:T(8,128)} %fusion.68, bf16[2,1536,384]{2,1,0:T(8,128)(2,1)} %param.8, bf16[2,16,16,384]{3,2,1,0:T(8,128)(2,1)S(1)} %bitcast.77), kind=kOutput, calls=%fused_computation.39 | convolution fusion | flops 611942400 | bytes 6684672 | tf_op jit(solution)/shard_map/jrf,jdf->jrd/dot_general | solution.py:51
  50.2 2.9 %fusion.31 = bf16[2,16,8,384]{3,2,1,0:T(8,128)(2,1)S(1)} fusion(bf16[2,1536,384]{2,1,0:T(8,128)(2,1)} %param.8, f32[2,128,1536]{2,1,0:T(8,128)} %fusion.68), kind=kOutput, calls=%fused_computation.38 | convolution fusion | flops 305627136 | bytes 4128768 | tf_op jit(solution)/shard_map/jrf,jfd->jrd/dot_general | solution.py:50
  53.2 1.2 copy.42
  54.3 3.8 %all-to-all-start.1 = ((bf16[2,256,384]{2,0,1:T(2,128)(2,1)}), bf16[2,256,384]{2,0,1:T(2,128)(2,1)S(1)}, u32[]{:S(2)}, u32[]{:S(2)}) async-start(bf16[2,256,384]{2,0,1:T(2,128)(2,1)} %bitcast.79), calls=%async_computation.1 | async-start | bytes 786432 | tf_op jit(solution)/shard_map/all_to_all | solution.py:16
  58.1 1.6 %fusion.22 = f32[2,256,768]{2,1,0:T(8,128)S(1)} fusion(bf16[2,384,1536]{2,1,0:T(8,128)(2,1)S(1)} %copy-done, s32[]{:T(128)S(6)} %select_n.4, bf16[2,32,16,384]{3,2,1,0:T(8,128)(2,1)} %all_gather.3), kind=kOutput, calls=%fused_computation.29 | convolution fusion | flops 301989888 | bytes 3145732 | tf_op jit(solution)/shard_map/jrd,jdf->jrf/dot_general | solution.py:43
  59.8 1.1 copy-done.6
  60.9 2.2 %fusion.45 = f32[2,768,384]{2,1,0:T(8,128)} fusion(f32[2,256,768]{2,1,0:T(8,128)S(1)} %fusion.22, bf16[2,32,16,384]{3,2,1,0:T(8,128)(2,1)S(1)} %copy-done.3), kind=kOutput, calls=%fused_computation.56 | convolution fusion | flops 305528832 | bytes 4325376 | tf_op jit(solution)/shard_map/jrf,jrd->jfd/dot_general | solution.py:65
  63.1 5.1 %fusion.29 = f32[2,384,768]{2,1,0:T(8,128)} fusion(f32[2,256,768]{2,1,0:T(8,128)} %copy-done.6, bf16[2,1536,384]{2,1,0:T(8,128)(2,1)} %param.8, s32[]{:T(128)S(6)} %select_n.4, bf16[2,32,16,384]{3,2,1,0:T(8,128)(2,1)} %all_gather.3), kind=kOutput, calls=%fused_computation.33 | convolution fusion | flops 611844096 | bytes 5898244 | tf_op jit(solution)/shard_map/jrd,jrf->jdf/dot_general | solution.py:64
  68.2 2.1 %all-to-all-done.1 = bf16[2,256,384]{2,0,1:T(2,128)(2,1)S(1)} async-done(((bf16[2,256,384]{2,0,1:T(2,128)(2,1)}), bf16[2,256,384]{2,0,1:T(2,128)(2,1)S(1)}, u32[]{:S(2)}, u32[]{:S(2)}) %all-to-all-start.1) | async-done | bytes 393248 | tf_op jit(solution)/shard_map/all_to_all | solution.py:16
  70.3 0.4 copy.44
  70.7 0.9 all_to_all.30
  71.6 2.8 %fusion.38 = f32[8,32,196]{2,1,0:T(8,128)} fusion(bf16[32,16,384]{2,0,1:T(8,128)(2,1)} %all_to_all.30, bf16[8,196,384]{2,0,1:T(8,128)(2,1)} %param.5), kind=kOutput, calls=%fused_computation.46 | convolution fusion | flops 38535168 | bytes 1798144 | tf_op jit(solution)/shard_map/bpd,sbd->bps/dot_general | solution.py:68
  74.4 0.6 fusion.35
  75.0 0.3 copy-done.10
  75.3 2.1 %fusion.65 = f32[8,196,384]{2,1,0:T(8,128)} fusion(bf16[8,196,32]{1,2,0:T(8,128)(2,1)S(1)} %copy-done.10, bf16[32,16,384]{2,0,1:T(8,128)(2,1)S(1)} %copy-done.11), kind=kOutput, calls=%fused_computation.81 | convolution fusion | flops 38535168 | bytes 2736128 | tf_op jit(solution)/shard_map/bps,sbd->bpd/dot_general | solution.py:76
  77.4 2.2 %copy.47 = f32[8,32,196]{1,0,2:T(8,128)} copy(f32[8,32,196]{2,1,0:T(8,128)} %fusion.38) | data formatting | bytes 401408 | tf_op jit(solution)/shard_map/bpd,sbd->bps/dot_general | solution.py:68
  79.6 1.4 %fusion.43 = f32[8,32]{1,0:T(8,128)S(1)} fusion(f32[8,32,196]{1,0,2:T(8,128)} %copy.47, f32[8,32]{1,0:T(8,128)S(1)} %copy-done.19, f32[8,196,32]{2,0,1:T(8,128)S(1)} %get-tuple-element.17, f32[8,32]{1,0:T(8,128)S(1)} %copy-done.17), kind=kLoop, calls=%fused_computation.53 | loop fusion | flops 200448 | bytes 404480 | tf_op jit(solution)/shard_map/reduce_sum | solution.py:70
  81.0 1.3 copy.49
  82.3 10.8 %fusion.21 = bf16[8,196,32]{2,0,1:T(8,128)(2,1)S(1)} fusion(f32[8,32,196]{1,0,2:T(8,128)} %copy.49, f32[8,32,196]{1,0,2:T(8,128)} %copy.47, f32[8,32]{1,0:T(8,128)S(1)} %fusion.43, f32[8,196,32]{2,0,1:T(8,128)} %get-tuple-element.19, f32[8,196]{0,1:T(8,128)S(1)} %copy-done.13, f32[8,32]{1,0:T(8,128)S(1)} %copy-done.19, ...), kind=kOutput, calls=%fused_computation.28 | output fusion | flops 553535 | bytes 912512 | tf_op jit(solution)/shard_map/sub | solution.py:73
  93.1 0.7 copy-done.4
  93.8 0.3 convolution_bitcast_fusion
  94.2 39.9 %psum.7 = f32[384,32]{0,1:T(8,128)} all-reduce(f32[384,32]{0,1:T(8,128)S(1)} %convolution_bitcast_fusion), channel_id=1, replica_groups=mesh['expert'=16,'dp'=2] {'expert','dp'}, use_global_device_ids=true, to_apply=%region_6.0 | all-reduce | flops 12288 | bytes 98304 | tf_op jit(solution)/shard_map/psum | solution.py:20
  134.1 2.4 %add_convert_fusion = bf16[8,196,384]{2,1,0:T(8,128)(2,1)S(1)} fusion(f32[8,196,384]{2,1,0:T(8,128)} %fusion.65, bf16[8,196,32]{2,0,1:T(8,128)(2,1)} %copy-done.4, bf16[384,32]{0,1:T(8,128)(2,1)S(1)} %copy-done.15), kind=kOutput, calls=%fused_computation.2 | convolution fusion | flops 39739392 | bytes 3737600 | tf_op jit(solution)/shard_map/bps,ds->bpd/dot_general | solution.py:77
  136.5 1.2 copy.55
  (30 shorter events, 0.2 us)
Async XLA Ops:
  0.6 43.1 %copy-start = (bf16[2,384,1536]{2,1,0:T(8,128)(2,1)S(1)}, bf16[2,384,1536]{2,1,0:T(8,128)(2,1)}, u32[]{:S(2)}) copy-start(bf16[2,384,1536]{2,1,0:T(8,128)(2,1)} %param.7) | copy-start | bytes 7077892
  2.5 1.4 %copy-start.16 = (f32[8,32]{1,0:T(8,128)}, f32[8,32]{1,0:T(8,128)S(1)}, u32[]{:S(2)}) copy-start(f32[8,32]{1,0:T(8,128)S(1)} %get-tuple-element.16) | copy-start | bytes 3076
  3.7 4.9 %copy-start.12 = (f32[8,196]{0,1:T(8,128)}, f32[8,196]{0,1:T(8,128)S(1)}, u32[]{:S(2)}) copy-start(f32[8,196]{0,1:T(8,128)S(1)} %get-tuple-element.18) | copy-start | bytes 18820
  4.0 0.6 copy-start.18
  6.7 2.8 %copy-start.9 = (bf16[8,196,32]{1,2,0:T(8,128)(2,1)}, bf16[8,196,32]{1,2,0:T(8,128)(2,1)S(1)}, u32[]{:S(2)}) copy-start(bf16[8,196,32]{1,2,0:T(8,128)(2,1)S(1)} %copy.45) | copy-start | bytes 301060
  6.7 2.0 %copy-start.2 = (f32[8,196,32]{2,0,1:T(8,128)S(1)}, f32[8,196,32]{2,0,1:T(8,128)}, u32[]{:S(2)}) copy-start(f32[8,196,32]{2,0,1:T(8,128)} %get-tuple-element.19) | copy-start | bytes 602116
  6.7 2.2 %copy-start.7 = (bf16[8,196,384]{2,0,1:T(8,128)(2,1)S(1)}, bf16[8,196,384]{2,0,1:T(8,128)(2,1)}, u32[]{:S(2)}) copy-start(bf16[8,196,384]{2,0,1:T(8,128)(2,1)} %param.9) | copy-start | bytes 3612676
  10.4 19.6 %all-to-all-start = ((bf16[32,16,384]{2,1,0:T(8,128)(2,1)}), bf16[32,16,384]{2,1,0:T(8,128)(2,1)S(1)}, u32[]{:S(2)}, u32[]{:S(2)}) async-start(bf16[32,16,384]{2,1,0:T(8,128)(2,1)} %copy.40), calls=%async_computation | async-start | bytes 786432 | tf_op jit(solution)/shard_map/all_to_all | solution.py:10
  30.0 0.7 copy-start.5
  50.2 2.9 %copy-start.14 = (bf16[2,16,8,384]{3,2,1,0:T(8,128)(2,1)S(1)}, bf16[2,16,8,384]{3,2,1,0:T(8,128)(2,1)}, u32[]{:S(2)}) copy-start(bf16[2,16,8,384]{3,2,1,0:T(8,128)(2,1)} %fusion.32) | copy-start | bytes 589828
  54.3 15.9 %all-to-all-start.1 = ((bf16[2,256,384]{2,0,1:T(2,128)(2,1)}), bf16[2,256,384]{2,0,1:T(2,128)(2,1)S(1)}, u32[]{:S(2)}, u32[]{:S(2)}) async-start(bf16[2,256,384]{2,0,1:T(2,128)(2,1)} %bitcast.79), calls=%async_computation.1 | async-start | bytes 786432 | tf_op jit(solution)/shard_map/all_to_all | solution.py:16
  58.1 2.8 %copy-start.3 = (bf16[2,32,16,384]{3,2,1,0:T(8,128)(2,1)S(1)}, bf16[2,32,16,384]{3,2,1,0:T(8,128)(2,1)}, u32[]{:S(2)}) copy-start(bf16[2,32,16,384]{3,2,1,0:T(8,128)(2,1)} %all_gather.3) | copy-start | bytes 2359300
  59.8 1.2 copy-start.6
  71.6 2.8 %copy-start.8 = (bf16[8,196,384]{2,0,1:T(8,128)(2,1)S(1)}, bf16[8,196,384]{2,0,1:T(8,128)(2,1)}, u32[]{:S(2)}) copy-start(bf16[8,196,384]{2,0,1:T(8,128)(2,1)} %param.9) | copy-start | bytes 3612676
  71.6 2.8 %copy-start.11 = (bf16[32,16,384]{2,0,1:T(8,128)(2,1)S(1)}, bf16[32,16,384]{2,0,1:T(8,128)(2,1)}, u32[]{:S(2)}) copy-start(bf16[32,16,384]{2,0,1:T(8,128)(2,1)} %all_to_all.30) | copy-start | bytes 1179652
  74.4 0.9 copy-start.10
  75.3 4.3 %copy-start.17 = (f32[8,32]{1,0:T(8,128)S(1)}, f32[8,32]{1,0:T(8,128)}, u32[]{:S(2)}) copy-start(f32[8,32]{1,0:T(8,128)} %copy-done.16) | copy-start | bytes 3076
  75.3 4.3 %copy-start.19 = (f32[8,32]{1,0:T(8,128)S(1)}, f32[8,32]{1,0:T(8,128)}, u32[]{:S(2)}) copy-start(f32[8,32]{1,0:T(8,128)} %copy-done.18) | copy-start | bytes 3076
  79.6 2.7 %copy-start.13 = (f32[8,196]{0,1:T(8,128)S(1)}, f32[8,196]{0,1:T(8,128)}, u32[]{:S(2)}) copy-start(f32[8,196]{0,1:T(8,128)} %copy-done.12) | copy-start | bytes 18820
  82.3 11.6 %copy-start.1 = (bf16[8,196,384]{2,0,1:T(8,128)(2,1)S(1)}, bf16[8,196,384]{2,0,1:T(8,128)(2,1)}, u32[]{:S(2)}) copy-start(bf16[8,196,384]{2,0,1:T(8,128)(2,1)} %param.5) | copy-start | bytes 3612676
  93.1 0.8 copy-start.4
  93.8 40.2 %copy-start.15 = (bf16[384,32]{0,1:T(8,128)(2,1)S(1)}, bf16[384,32]{0,1:T(8,128)(2,1)}, u32[]{:S(2)}) copy-start(bf16[384,32]{0,1:T(8,128)(2,1)} %param.6) | copy-start | bytes 73732

commit v2 on v1

--- a/solution.py
+++ b/solution.py
@@ -3,21 +3,158 @@
 import jax
 import jax.numpy as jnp
 from jax import lax
+from jax.experimental import pallas as pl
+from jax.experimental.pallas import tpu as pltpu
 from jax.sharding import PartitionSpec as P
 
+MESH = pl.DeviceIdType.MESH
+
+
+def greet(n):
+    me = lax.axis_index("expert")
+    barrier = pltpu.get_barrier_semaphore()
+
+    @pl.loop(1, n)
+    def _(k):
+        pl.semaphore_signal(
+            barrier, inc=1, device_id={"expert": lax.rem(me + k, n)}, device_id_type=MESH
+        )
+
+    return me, barrier
+
+
+def exchange_kernel(n, outward, x_ref, y_ref, send_sem, recv_sem, own_sem):
+    me, barrier = greet(n)
+
+    def block(peer):
+        return x_ref.at[peer] if outward else x_ref.at[:, peer]
+
+    landing = y_ref.at[:, me] if outward else y_ref.at[me]
+    own = pltpu.make_async_copy(block(me), landing, own_sem)
+    own.start()
+    pl.semaphore_wait(barrier, n - 1)
+
+    def copy(k):
+        peer = lax.rem(me + k, n)
+        return pltpu.make_async_remote_copy(
+            src_ref=block(peer),
+            dst_ref=landing,
+            send_sem=send_sem.at[k],
+            recv_sem=recv_sem.at[k],
+            device_id={"expert": peer},
+            device_id_type=MESH,
+        )
+
+    @pl.loop(1, n)
+    def _(k):
+        copy(k).start()
+
+    own.wait()
+
+    @pl.loop(1, n)
+    def _(k):
+        copy(k).wait()
+
+
+def exchange(x, n, shape, outward, collective_id):
+    return pl.pallas_call(
+        functools.partial(exchange_kernel, n, outward),
+        out_shape=jax.ShapeDtypeStruct(shape, x.dtype),
+        in_specs=[pl.BlockSpec(memory_space=pltpu.VMEM)],
+        out_specs=pl.BlockSpec(memory_space=pltpu.VMEM),
+        scratch_shapes=[
+            pltpu.SemaphoreType.DMA((n,)),
+            pltpu.SemaphoreType.DMA((n,)),
+            pltpu.SemaphoreType.DMA,
+        ],
+        compiler_params=pltpu.CompilerParams(
+            collective_id=collective_id, has_side_effects=True
+        ),
+    )(x)
+
 
 def to_experts(x, n):
-    wide = lax.all_to_all(x, "expert", split_axis=0, concat_axis=1, tiled=True)
-    return wide.reshape(wide.shape[0], n, x.shape[1], x.shape[2])
+    each = x.shape[0] // n
+    x = x.reshape(n, each, x.shape[1], x.shape[2])
+    return exchange(x, n, (each, n, x.shape[2], x.shape[3]), True, 0)
 
 
 def to_images(x, n):
-    flat = x.reshape(x.shape[0], n * x.shape[2], x.shape[3])
-    return lax.all_to_all(flat, "expert", split_axis=1, concat_axis=0, tiled=True)
+    y = exchange(x, n, (n, x.shape[0], x.shape[2], x.shape[3]), False, 1)
+    return y.reshape(n * x.shape[0], x.shape[2], x.shape[3])
+
+
+def sum_kernel(n, dp, x_ref, y_ref, terms, halves, total, send_a, recv_a, send_b, recv_b, send_c, recv_c):
+    me, barrier = greet(n)
+    row = lax.axis_index("dp")
+
+    @pl.loop(1, dp)
+    def _(k):
+        pl.semaphore_signal(
+            barrier, inc=1, device_id={"dp": lax.rem(row + k, dp)}, device_id_type=MESH
+        )
+
+    pl.semaphore_wait(barrier, n + dp - 2)
+
+    def send(src, dst, sends, recvs, k, axis, place, size):
+        return pltpu.make_async_remote_copy(
+            src_ref=src,
+            dst_ref=dst,
+            send_sem=sends.at[k],
+            recv_sem=recvs.at[k],
+            device_id={axis: lax.rem(place + k, size)},
+            device_id_type=MESH,
+        )
+
+    def first(k):
+        return send(x_ref.at[lax.rem(me + k, n)], terms.at[me], send_a, recv_a, k, "expert", me, n)
+
+    def second(k):
+        return send(halves.at[row], halves.at[row], send_b, recv_b, k, "dp", row, dp)
+
+    def third(k):
+        return send(total, y_ref.at[me], send_c, recv_c, k, "expert", me, n)
+
+    def run(copy, size):
+        @pl.loop(1, size)
+        def _(k):
+            copy(k).start()
+
+        @pl.loop(1, size)
+        def _(k):
+            copy(k).wait()
+
+    terms[me] = x_ref[me]
+    run(first, n)
+    halves[row] = jnp.sum(terms[...], axis=0)
+    run(second, dp)
+    total[...] = jnp.sum(halves[...], axis=0)
+    y_ref[me] = total[...]
+    run(third, n)
 
 
 def sum_all(x, n, dp):
-    return lax.psum(x, ("expert", "dp"))
+    each = x.shape[0] // n
+    block = (each, x.shape[1])
+    y = pl.pallas_call(
+        functools.partial(sum_kernel, n, dp),
+        out_shape=jax.ShapeDtypeStruct((n,) + block, x.dtype),
+        in_specs=[pl.BlockSpec(memory_space=pltpu.VMEM)],
+        out_specs=pl.BlockSpec(memory_space=pltpu.VMEM),
+        scratch_shapes=[
+            pltpu.VMEM((n,) + block, x.dtype),
+            pltpu.VMEM((dp,) + block, x.dtype),
+            pltpu.VMEM(block, x.dtype),
+            pltpu.SemaphoreType.DMA((n,)),
+            pltpu.SemaphoreType.DMA((n,)),
+            pltpu.SemaphoreType.DMA((dp,)),
+            pltpu.SemaphoreType.DMA((dp,)),
+            pltpu.SemaphoreType.DMA((n,)),
+            pltpu.SemaphoreType.DMA((n,)),
+        ],
+        compiler_params=pltpu.CompilerParams(collective_id=2, has_side_effects=True),
+    )(x.reshape((n,) + block))
+    return y.reshape(x.shape)
 
 
 def on_device(n, dp, tokens, router, expert_in, expert_out, out_grad):

time: 138 us -> 106 us (0.77)
  Pallas kernels: 0 us -> 49.7 us
  blocking collectives: 51.8 us -> 11.7 us
  waiting for transfers between devices: 14.3 us -> 0 us
  other arithmetic: 14.9 us -> 1.69 us
  starting transfers between devices: 11.2 us -> 0 us
  local copies, waits for them, and re-layouts: 13.9 us -> 7.05 us
  matrix products: 30.8 us -> 34.4 us
    pallas_call x0 -> x3, Pallas kernels: none -> 49.7 us  [the longest x2 30.2 us: exchange(): pl.pallas_call(functools.partial(exchange_kernel, n, outward), out_shape=...]
    psum x1 -> x0, blocking collectives: 39.9 us -> none  [sum_all(): return lax.psum(x, ('expert', 'dp'))]
    all_to_all x2 -> x0, waiting for transfers between devices: 14.3 us -> none  [the longest x1 12.2 us: to_experts(): wide = lax.all_to_all(x, 'expert', split_axis=0, concat_axis=1, tiled=True)]
    all_to_all x2 -> x0, starting transfers between devices: 11.2 us -> none  [the longest x1 7.39 us: to_experts(): wide = lax.all_to_all(x, 'expert', split_axis=0, concat_axis=1, tiled=True)]
    sub x1, other arithmetic: 10.8 us -> 0.64 us  [on_device(): combine_grad - jnp.sum(combine * combine_grad, axis=2, keepdims=True)]
    dot_general x2 -> x1, local copies, waits for them, and re-layouts: 3.46 us -> 0.36 us  [on_device(): logits = dot('bpd,ds->bps', tokens, router)]
    all_to_all x4 -> x0, local copies, waits for them, and re-layouts: 2.38 us -> none  [the longest x3 1.34 us: to_images(): lax.all_to_all(flat, 'expert', split_axis=1, concat_axis=0, tiled=True)]
    dot_general x1, matrix products: 2.81 us -> 0.6 us  [on_device(): dispatch_grad = dot('bpd,sbd->bps', tokens, inputs_grad)]
  transfers between devices with their start and end apart: 2 -> 0, of which waited for: 2 -> 0; matrix products, arithmetic and copies ran while one was open for 6% -> 0% of each run, Pallas kernels for 0% -> 0%
where the time goes in v2:
time: 106 us; the launch traced here: 105 us
  Pallas kernels  49.7 us (47%)
  matrix products  34.4 us (32%)
  blocking collectives  11.7 us (11%)
  local copies, waits for them, and re-layouts  7.05 us (7%)
  other arithmetic  1.69 us (2%)
    pallas_call x2, Pallas kernels, exchange(): pl.pallas_call(functools.partial(exchange_kernel, n, outward), out_shape=...  30.2 us
    pallas_call x1, Pallas kernels, sum_all(): pl.pallas_call(functools.partial(sum_kernel, n, dp), out_shape=jax.ShapeD...  19.5 us
    all_gather x1, blocking collectives, on_device(): everyone = lax.all_gather(here, 'dp', axis=1, tiled=True)  11.7 us
    dot_general x1, matrix products, on_device(): grad_in = dot('jrd,jrf->jdf', slots_all, hidden_grad_all)  4.82 us
    dot_general x1, matrix products, on_device(): input_grad_here = dot('jrf,jdf->jrd', hidden_grad, expert_in).astype(low)  4.09 us
    dot_general x1, matrix products, on_device(): second_part = dot('bps,ds->bpd', logit_low, router)  3.83 us
    dot_general x1, matrix products, on_device(): grad_out = dot('jrf,jrd->jfd', activated_all, grads_all)  3.57 us
    dot_general x2, matrix products, hidden_side(): hidden = dot('jrd,jdf->jrf', inputs, first)  3.44 us

profile of v2, /device:TPU:0, one launch (start us, length us, event | category | flops | bytes accessed | tf_op | source)
XLA Modules:
  0.0 105.4 jit_solution(10623475285467844806)
XLA Ops:
  0.6 0.0 copy-start
  0.6 2.0 %fusion.120 = (f32[8,32]{1,0:T(8,128)S(1)}, f32[8,196]{0,1:T(8,128)S(1)}, f32[8,196,32]{2,0,1:T(8,128)S(1)}) fusion(bf16[8,196,384]{2,0,1:T(8,128)(2,1)} %param.5, bf16[384,32]{0,1:T(8,128)(2,1)} %param.6), kind=kOutput, calls=%fused_computation.120 | convolution fusion | flops 38633696 | bytes 1436800 | tf_op jit(solution)/shard_map/bpd,ds->bps/dot_general | solution.py:164
  2.7 0.1 copy.26
  2.7 0.4 copy.22
  3.1 0.0 copy-start.1
  3.1 0.2 fusion.63
  3.3 1.9 %fusion.34 = bf16[32,8,384]{2,0,1:T(8,128)(2,1)S(1)} fusion(bf16[8,196,384]{2,0,1:T(8,128)(2,1)} %param.9, f32[8,196,32]{1,2,0:T(8,128)S(1)} %copy.22, f32[8,196]{1,0:T(8,128)S(1)} %get-tuple-element.11, f32[8,196]{1,0:T(8,128)S(1)} %copy.26), kind=kOutput, calls=%fused_computation.43 | convolution fusion | flops 38784000 | bytes 1614080 | tf_op jit(solution)/shard_map/bps,bpd->sbd/dot_general | solution.py:170
  5.1 0.0 copy-done.1
  5.2 0.5 fusion.33
  5.7 0.1 pad_maximum_fusion
  5.7 0.9 copy.12
  6.6 14.9 %shard_map.84 = bf16[2,16,16,384]{3,2,1,0:T(8,128)(2,1)} custom-call(bf16[16,2,16,384]{3,2,1,0:T(8,128)(2,1)} %bitcast.49), custom_call_target="tpu_custom_call" | custom-call | tf_op jit(solution)/shard_map/pallas_call | solution.py:60
  21.6 11.7 %all_gather.3 = bf16[2,32,16,384]{3,2,1,0:T(8,128)(2,1)S(1)} all-gather(bf16[2,16,16,384]{3,2,1,0:T(8,128)(2,1)} %shard_map.84), channel_id=1, replica_groups=mesh['expert'=16,'dp'=2] {'dp'}, dimensions={1}, use_global_device_ids=true | all-gather | bytes 1179648 | tf_op jit(solution)/shard_map/all_gather | solution.py:173
  33.3 0.0 copy-done
  33.3 0.0 copy-start.4
  33.3 0.0 copy-start.3
  33.3 1.7 %fusion.16 = f32[2,256,768]{2,1,0:T(8,128)} fusion(bf16[2,384,1536]{2,1,0:T(8,128)(2,1)S(1)} %copy-done, s32[]{:T(128)S(6)} %select_n.4, bf16[2,32,16,384]{3,2,1,0:T(8,128)(2,1)S(1)} %all_gather.3), kind=kOutput, calls=%fused_computation.23 | convolution fusion | flops 301989888 | bytes 3145732 | tf_op jit(solution)/shard_map/jrd,jdf->jrf/dot_general | solution.py:180
  35.0 0.0 copy-done.4
  35.0 0.0 copy-done.3
  35.0 1.7 %fusion.73 = f32[2,128,1536]{2,1,0:T(8,128)} fusion(bf16[2,384,1536]{2,1,0:T(8,128)(2,1)S(1)} %copy-done, bf16[2,16,16,384]{3,2,1,0:T(8,128)(2,1)S(1)} %copy-done.3), kind=kOutput, calls=%fused_computation.83 | convolution fusion | flops 301989888 | bytes 4128768 | tf_op jit(solution)/shard_map/jrd,jdf->jrf/dot_general | solution.py:180
  36.8 4.1 %fusion.32 = bf16[2,16,8,384]{3,2,1,0:T(8,128)(2,1)S(1)} fusion(bf16[2,384,1536]{2,1,0:T(8,128)(2,1)S(1)} %copy-done, f32[2,128,1536]{2,1,0:T(8,128)} %fusion.73, bf16[2,1536,384]{2,1,0:T(8,128)(2,1)} %param.8, bf16[2,16,16,384]{3,2,1,0:T(8,128)(2,1)S(1)} %copy-done.3), kind=kOutput, calls=%fused_computation.41 | convolution fusion | flops 611942400 | bytes 6684672 | tf_op jit(solution)/shard_map/jrf,jdf->jrd/dot_general | solution.py:188
  40.9 2.9 %fusion.31 = bf16[2,16,8,384]{3,2,1,0:T(8,128)(2,1)S(1)} fusion(bf16[2,1536,384]{2,1,0:T(8,128)(2,1)} %param.8, f32[2,128,1536]{2,1,0:T(8,128)} %fusion.73), kind=kOutput, calls=%fused_computation.40 | convolution fusion | flops 305627136 | bytes 4128768 | tf_op jit(solution)/shard_map/jrf,jfd->jrd/dot_general | solution.py:187
  43.7 0.8 pad_maximum_fusion.1.x_ref
  44.5 15.3 %shard_map.85 = bf16[16,2,16,384]{3,2,1,0:T(8,128)(2,1)} custom-call(bf16[2,16,16,384]{3,2,1,0:T(8,128)(2,1)} %pad_maximum_fusion.1.x_ref), custom_call_target="tpu_custom_call" | custom-call | tf_op jit(solution)/shard_map/pallas_call | solution.py:60
  59.8 1.1 %fusion.121 = (bf16[32,8,384]{2,1,0:T(8,128)(2,1)S(1)}, bf16[32,8,384]{2,1,0:T(8,128)(2,1)S(1)}) fusion(bf16[32,16,384]{2,1,0:T(8,128)(2,1)} %bitcast.48), kind=kLoop, calls=%fused_computation.121 | loop fusion | bytes 786432 | tf_op jit(solution)/shard_map/slice | solution.py:193
  60.9 0.0 copy-start.2
  60.9 2.0 %convolution_bitcast_fusion = f32[8,196,32]{1,2,0:T(8,128)S(1)} fusion(bf16[8,196,384]{2,0,1:T(8,128)(2,1)} %param.9, bf16[32,8,384]{2,1,0:T(8,128)(2,1)S(1)} %get-tuple-element.12), kind=kOutput, calls=%fused_computation.37 | convolution fusion | flops 38535168 | bytes 1601536 | tf_op jit(solution)/shard_map/bpd,sbd->bps/dot_general | solution.py:204
  62.9 0.6 fusion.29
  63.5 0.0 copy-done.2
  63.5 0.6 convolution_bitcast_fusion.1
  64.1 2.4 %convolution_bitcast_fusion.2 = f32[32,384]{1,0:T(8,128)S(1)} fusion(f32[8,196,32]{1,2,0:T(8,128)S(1)} %fusion.29, f32[8,196,32]{1,2,0:T(8,128)S(1)} %convolution_bitcast_fusion.1, bf16[8,196,384]{2,0,1:T(8,128)(2,1)} %param.5, f32[8,196,32]{1,2,0:T(8,128)S(1)} %copy.22, f32[8,32]{1,0:T(8,128)S(1)} %get-tuple-element.10, f32[8,32]{1,0:T(8,128)S(1)} %get-tuple-element.8), kind=kOutput, calls=%fused_computation.44 | convolution fusion | flops 38987204 | bytes 1857536 | tf_op jit(solution)/shard_map/bps,bpd->sd/dot_general | solution.py:216
  66.5 0.7 reshape.52.x_ref
  67.2 0.0 copy-start.6
  67.2 19.5 %shard_map.86 = f32[16,2,384]{2,1,0:T(2,128)} custom-call(f32[16,2,384]{2,1,0:T(2,128)} %reshape.52.x_ref), custom_call_target="tpu_custom_call" | custom-call | tf_op jit(solution)/shard_map/pallas_call | solution.py:139
  86.7 1.5 %reshape.53 = f32[32,384]{1,0:T(8,128)} reshape(f32[16,2,384]{2,1,0:T(2,128)} %shard_map.86) | data formatting | bytes 98304 | tf_op jit(solution)/shard_map/reshape | solution.py:157
  88.1 2.5 %fusion.79 = f32[8,196,384]{2,1,0:T(8,128)} fusion(bf16[32,8,384]{2,1,0:T(8,128)(2,1)S(1)} %get-tuple-element.13, f32[8,196,32]{1,2,0:T(8,128)S(1)} %copy.22, f32[8,32]{1,0:T(8,128)S(1)} %get-tuple-element.10, f32[8,32]{1,0:T(8,128)S(1)} %get-tuple-element.8), kind=kOutput, calls=%fused_computation.88 | convolution fusion | flops 38685696 | bytes 2807808 | tf_op jit(solution)/shard_map/bps,sbd->bpd/dot_general | solution.py:213
  90.6 0.0 copy-done.6
  90.6 3.8 %add_convert_fusion = bf16[8,196,384]{2,1,0:T(8,128)(2,1)} fusion(f32[8,196,384]{2,1,0:T(8,128)} %fusion.79, f32[8,196,32]{1,2,0:T(8,128)S(1)} %fusion.29, f32[8,196,32]{1,2,0:T(8,128)S(1)} %convolution_bitcast_fusion.1, bf16[384,32]{0,1:T(8,128)(2,1)S(1)} %copy-done.6, f32[8,196,32]{1,2,0:T(8,128)S(1)} %copy.22, f32[8,32]{1,0:T(8,128)S(1)} %get-tuple-element.10, ...), kind=kOutput, calls=%fused_computation.2 | convolution fusion | flops 40191428 | bytes 4241408 | tf_op jit(solution)/shard_map/bps,ds->bpd/dot_general | solution.py:214
  94.4 0.0 copy-start.5
  94.4 2.5 %copy.20 = bf16[8,196,384]{2,0,1:T(8,128)(2,1)} copy(bf16[8,196,384]{2,1,0:T(8,128)(2,1)} %add_convert_fusion) | data formatting | bytes 2408448
  97.0 0.0 copy-done.5
  97.0 4.8 %fusion.23 = f32[2,384,768]{2,1,0:T(8,128)} fusion(f32[2,256,768]{2,1,0:T(8,128)} %fusion.16, bf16[2,1536,384]{2,1,0:T(8,128)(2,1)} %param.8, s32[]{:T(128)S(6)} %select_n.4, bf16[2,32,16,384]{3,2,1,0:T(8,128)(2,1)S(1)} %copy-done.5), kind=kOutput, calls=%fused_computation.27 | convolution fusion | flops 611844096 | bytes 5898244 | tf_op jit(solution)/shard_map/jrd,jrf->jdf/dot_general | solution.py:201
  101.8 3.6 %fusion.41 = f32[2,768,384]{2,1,0:T(8,128)} fusion(f32[2,256,768]{2,1,0:T(8,128)} %fusion.16, bf16[2,32,16,384]{3,2,1,0:T(8,128)(2,1)S(1)} %copy-done.5), kind=kOutput, calls=%fused_computation.50 | convolution fusion | flops 305528832 | bytes 4325376 | tf_op jit(solution)/shard_map/jrf,jrd->jfd/dot_general | solution.py:202
Async XLA Ops:
  0.6 32.7 %copy-start = (bf16[2,384,1536]{2,1,0:T(8,128)(2,1)S(1)}, bf16[2,384,1536]{2,1,0:T(8,128)(2,1)}, u32[]{:S(2)}) copy-start(bf16[2,384,1536]{2,1,0:T(8,128)(2,1)} %param.7) | copy-start | bytes 7077892
  3.1 2.1 %copy-start.1 = (bf16[8,196,384]{2,0,1:T(8,128)(2,1)S(1)}, bf16[8,196,384]{2,0,1:T(8,128)(2,1)}, u32[]{:S(2)}) copy-start(bf16[8,196,384]{2,0,1:T(8,128)(2,1)} %param.5) | copy-start | bytes 3612676
  33.3 1.7 %copy-start.4 = (bf16[2,32,16,384]{3,2,1,0:T(8,128)(2,1)}, bf16[2,32,16,384]{3,2,1,0:T(8,128)(2,1)S(1)}, u32[]{:S(2)}) copy-start(bf16[2,32,16,384]{3,2,1,0:T(8,128)(2,1)S(1)} %all_gather.3) | copy-start | bytes 2359300
  33.3 1.7 %copy-start.3 = (bf16[2,16,16,384]{3,2,1,0:T(8,128)(2,1)S(1)}, bf16[2,16,16,384]{3,2,1,0:T(8,128)(2,1)}, u32[]{:S(2)}) copy-start(bf16[2,16,16,384]{3,2,1,0:T(8,128)(2,1)} %shard_map.84) | copy-start | bytes 1179652
  60.9 2.6 %copy-start.2 = (bf16[8,196,384]{2,0,1:T(8,128)(2,1)S(1)}, bf16[8,196,384]{2,0,1:T(8,128)(2,1)}, u32[]{:S(2)}) copy-start(bf16[8,196,384]{2,0,1:T(8,128)(2,1)} %param.5) | copy-start | bytes 3612676
  67.2 23.4 %copy-start.6 = (bf16[384,32]{0,1:T(8,128)(2,1)S(1)}, bf16[384,32]{0,1:T(8,128)(2,1)}, u32[]{:S(2)}) copy-start(bf16[384,32]{0,1:T(8,128)(2,1)} %param.6) | copy-start | bytes 73732
  94.4 2.5 %copy-start.5 = (bf16[2,32,16,384]{3,2,1,0:T(8,128)(2,1)S(1)}, bf16[2,32,16,384]{3,2,1,0:T(8,128)(2,1)}, u32[]{:S(2)}) copy-start(bf16[2,32,16,384]{3,2,1,0:T(8,128)(2,1)} %copy-done.4) | copy-start | bytes 2359300

commit v3 on v2

--- a/solution.py
+++ b/solution.py
@@ -21,6 +21,18 @@
         )
 
     return me, barrier
+
+
+def greet_dp(dp, barrier):
+    row = lax.axis_index("dp")
+
+    @pl.loop(1, dp)
+    def _(k):
+        pl.semaphore_signal(
+            barrier, inc=1, device_id={"dp": lax.rem(row + k, dp)}, device_id_type=MESH
+        )
+
+    return row
 
 
 def exchange_kernel(n, outward, x_ref, y_ref, send_sem, recv_sem, own_sem):
@@ -79,21 +91,84 @@
     return exchange(x, n, (each, n, x.shape[2], x.shape[3]), True, 0)
 
 
-def to_images(x, n):
-    y = exchange(x, n, (n, x.shape[0], x.shape[2], x.shape[3]), False, 1)
-    return y.reshape(n * x.shape[0], x.shape[2], x.shape[3])
+def back_kernel(n, dp, x_ref, here_ref, y_ref, all_ref, send_sem, recv_sem, send_dp, recv_dp, own_sem):
+    me, barrier = greet(n)
+    row = greet_dp(dp, barrier)
+    place = all_ref.at[:, pl.ds(row * n, n)]
+    keep = pltpu.make_async_copy(here_ref, place, own_sem.at[0])
+    own = pltpu.make_async_copy(x_ref.at[:, me], y_ref.at[me], own_sem.at[1])
+    keep.start()
+    own.start()
+    pl.semaphore_wait(barrier, n + dp - 2)
+
+    def copy(k):
+        peer = lax.rem(me + k, n)
+        return pltpu.make_async_remote_copy(
+            src_ref=x_ref.at[:, peer],
+            dst_ref=y_ref.at[me],
+            send_sem=send_sem.at[k],
+            recv_sem=recv_sem.at[k],
+            device_id={"expert": peer},
+            device_id_type=MESH,
+        )
+
+    def across(k):
+        return pltpu.make_async_remote_copy(
+            src_ref=here_ref,
+            dst_ref=place,
+            send_sem=send_dp.at[k],
+            recv_sem=recv_dp.at[k],
+            device_id={"dp": lax.rem(row + k, dp)},
+            device_id_type=MESH,
+        )
+
+    @pl.loop(1, dp)
+    def _(k):
+        across(k).start()
+
+    @pl.loop(1, n)
+    def _(k):
+        copy(k).start()
+
+    keep.wait()
+    own.wait()
+
+    @pl.loop(1, n)
+    def _(k):
+        copy(k).wait()
+
+    @pl.loop(1, dp)
+    def _(k):
+        across(k).wait()
+
+
+def to_images(x, here, n, dp):
+    each, _, rows, width = x.shape
+    y, everyone = pl.pallas_call(
+        functools.partial(back_kernel, n, dp),
+        out_shape=(
+            jax.ShapeDtypeStruct((n, each, rows, width), x.dtype),
+            jax.ShapeDtypeStruct((each, dp * n, rows, width), x.dtype),
+        ),
+        in_specs=[pl.BlockSpec(memory_space=pltpu.VMEM)] * 2,
+        out_specs=(pl.BlockSpec(memory_space=pltpu.VMEM),) * 2,
+        scratch_shapes=[
+            pltpu.SemaphoreType.DMA((n,)),
+            pltpu.SemaphoreType.DMA((n,)),
+            pltpu.SemaphoreType.DMA((dp,)),
+            pltpu.SemaphoreType.DMA((dp,)),
+            pltpu.SemaphoreType.DMA((2,)),
+        ],
+        compiler_params=pltpu.CompilerParams(
+            collective_id=1, has_side_effects=True, vmem_limit_bytes=24 * 1024 * 1024
+        ),
+    )(x, here)
+    return y.reshape(n * each, rows, width), everyone
 
 
 def sum_kernel(n, dp, x_ref, y_ref, terms, halves, total, send_a, recv_a, send_b, recv_b, send_c, recv_c):
     me, barrier = greet(n)
-    row = lax.axis_index("dp")
-
-    @pl.loop(1, dp)
-    def _(k):
-        pl.semaphore_signal(
-            barrier, inc=1, device_id={"dp": lax.rem(row + k, dp)}, device_id_type=MESH
-        )
-
+    row = greet_dp(dp, barrier)
     pl.semaphore_wait(barrier, n + dp - 2)
 
     def send(src, dst, sends, recvs, k, axis, place, size):
@@ -170,7 +245,6 @@
     slot_grads = dot("bps,bpd->sbd", combine_low, out_grad).astype(low)
     here = to_experts(jnp.concatenate([slots, slot_grads], axis=1), n)
     each, width = here.shape[0], here.shape[3]
-    everyone = lax.all_gather(here, "dp", axis=1, tiled=True)
 
     def halves(block):
         flat = (each, block.shape[1] * images, width)
@@ -187,8 +261,11 @@
     outputs_here = dot("jrf,jfd->jrd", activated, expert_out).astype(low)
     input_grad_here = dot("jrf,jdf->jrd", hidden_grad, expert_in).astype(low)
     split = (each, n, images, width)
-    back = to_images(
-        jnp.concatenate([outputs_here.reshape(split), input_grad_here.reshape(split)], axis=2), n
+    back, everyone = to_images(
+        jnp.concatenate([outputs_here.reshape(split), input_grad_here.reshape(split)], axis=2),
+        here,
+        n,
+        dp,
     )
     outputs, inputs_grad = back[:, :images], back[:, images:]
 

time: 106 us -> 89.9 us (0.85)
  blocking collectives: 11.7 us -> 0 us
  matrix products: 34.4 us -> 32.1 us
  Pallas kernels: 49.7 us -> 47.9 us
    pallas_call x0 -> x1, Pallas kernels: none -> 17.4 us  [to_images(): pl.pallas_call(functools.partial(back_kernel, n, dp), out_shape=(jax.Shap...]
    pallas_call x2 -> x1, Pallas kernels: 30.2 us -> 14.9 us  [exchange(): pl.pallas_call(functools.partial(exchange_kernel, n, outward), out_shape=...]
    all_gather x1 -> x0, blocking collectives: 11.7 us -> none  [on_device(): everyone = lax.all_gather(here, 'dp', axis=1, tiled=True)]
    pallas_call x1, Pallas kernels: 19.5 us -> 15.6 us  [sum_all(): pl.pallas_call(functools.partial(sum_kernel, n, dp), out_shape=jax.ShapeD...]
    dot_general x1, matrix products: 2.85 us -> 0.71 us  [on_device(): outputs_here = dot('jrf,jfd->jrd', activated, expert_out).astype(low)]
    unnamed x16 -> x32, local copies, waits for them, and re-layouts: 2.64 us -> 4.04 us
    dot_general x1, matrix products: 1.97 us -> 0.6 us  [on_device(): combine_grad = dot('bpd,sbd->bps', out_grad, outputs)]
where the time goes in v3:
time: 89.9 us; the launch traced here: 89.4 us
  Pallas kernels  47.9 us (53%)
  matrix products  32.1 us (36%)
  local copies, waits for them, and re-layouts  7.43 us (8%)
  other arithmetic  1.09 us (1%)
    pallas_call x1, Pallas kernels, to_images(): pl.pallas_call(functools.partial(back_kernel, n, dp), out_shape=(jax.Shap...  17.4 us
    pallas_call x1, Pallas kernels, sum_all(): pl.pallas_call(functools.partial(sum_kernel, n, dp), out_shape=jax.ShapeD...  15.6 us
    pallas_call x1, Pallas kernels, exchange(): pl.pallas_call(functools.partial(exchange_kernel, n, outward), out_shape=...  14.9 us
    dot_general x1, matrix products, on_device(): grad_in = dot('jrd,jrf->jdf', slots_all, hidden_grad_all)  4.82 us
    dot_general x1, matrix products, on_device(): second_part = dot('bps,ds->bpd', logit_low, router)  4.09 us
    dot_general x1, matrix products, on_device(): input_grad_here = dot('jrf,jdf->jrd', hidden_grad, expert_in).astype(low)  4.08 us
    unnamed x32, local copies, waits for them, and re-layouts  4.04 us
    dot_general x1, matrix products, on_device(): grad_out = dot('jrf,jrd->jfd', activated_all, grads_all)  3.57 us

profile of v3, /device:TPU:0, one launch (start us, length us, event | category | flops | bytes accessed | tf_op | source)
XLA Modules:
  0.0 89.4 jit_solution(5015518058841734481)
XLA Ops:
  0.6 0.0 copy-start
  0.6 2.0 %fusion.130 = (f32[8,32]{1,0:T(8,128)S(1)}, f32[8,196]{0,1:T(8,128)S(1)}, f32[8,196,32]{2,0,1:T(8,128)S(1)}) fusion(bf16[8,196,384]{2,0,1:T(8,128)(2,1)} %param.5, bf16[384,32]{0,1:T(8,128)(2,1)} %param.6), kind=kOutput, calls=%fused_computation.126 | convolution fusion | flops 38633696 | bytes 1436800 | tf_op jit(solution)/shard_map/bpd,ds->bps/dot_general | solution.py:239
  2.7 0.1 copy.26
  2.7 0.4 copy.22
  3.1 0.0 copy-start.2
  3.1 0.2 fusion.73
  3.3 0.0 copy-start.12
  3.3 2.0 %fusion.34 = bf16[32,8,384]{2,0,1:T(8,128)(2,1)S(1)} fusion(bf16[8,196,384]{2,0,1:T(8,128)(2,1)} %param.9, f32[8,196,32]{1,2,0:T(8,128)S(1)} %copy.22, f32[8,196]{1,0:T(8,128)S(1)} %get-tuple-element.15, f32[8,196]{1,0:T(8,128)S(1)} %copy.26), kind=kOutput, calls=%fused_computation.43 | convolution fusion | flops 38784000 | bytes 1614080 | tf_op jit(solution)/shard_map/bps,bpd->sbd/dot_general | solution.py:245
  5.3 0.0 copy-done.2
  5.3 0.5 fusion.33
  5.8 0.0 copy-done.4
  5.8 0.0 copy-done.12
  5.9 0.9 copy.12
  6.7 14.9 %shard_map.84.here_ref = bf16[2,16,16,384]{3,2,1,0:T(8,128)(2,1)} custom-call(bf16[16,2,16,384]{3,2,1,0:T(8,128)(2,1)} %bitcast.51), custom_call_target="tpu_custom_call" | custom-call | tf_op jit(solution)/shard_map/pallas_call | solution.py:72
  21.7 0.0 copy-done
  21.7 0.0 copy-start.14
  21.7 1.6 %fusion.83 = f32[2,128,1536]{2,1,0:T(8,128)S(1)} fusion(bf16[2,384,1536]{2,1,0:T(8,128)(2,1)S(1)} %copy-done, bf16[2,16,16,384]{3,2,1,0:T(8,128)(2,1)} %shard_map.84.here_ref), kind=kOutput, calls=%fused_computation.89 | convolution fusion | flops 301989888 | bytes 4128768 | tf_op jit(solution)/shard_map/jrd,jdf->jrf/dot_general | solution.py:254
  23.4 0.0 copy-start.9
  23.4 1.1 %copy-done.9 = f32[2,128,1536]{2,1,0:T(8,128)} copy-done((f32[2,128,1536]{2,1,0:T(8,128)}, f32[2,128,1536]{2,1,0:T(8,128)S(1)}, u32[]{:S(2)}) %copy-start.9) | copy-done | bytes 1572888
  24.5 0.0 copy-done.14
  24.5 0.7 fusion.31
  25.2 0.3 copy-done.1
  25.5 4.1 %fusion.32 = bf16[2,16,8,384]{3,2,1,0:T(8,128)(2,1)S(1)} fusion(bf16[2,384,1536]{2,1,0:T(8,128)(2,1)S(1)} %copy-done, f32[2,128,1536]{2,1,0:T(8,128)} %copy-done.9, bf16[2,1536,384]{2,1,0:T(8,128)(2,1)} %param.8, bf16[2,16,16,384]{3,2,1,0:T(8,128)(2,1)S(1)} %copy-done.1), kind=kOutput, calls=%fused_computation.41 | convolution fusion | flops 611942400 | bytes 6684672 | tf_op jit(solution)/shard_map/jrf,jdf->jrd/dot_general | solution.py:262
  29.6 0.0 copy-start.10
  29.7 0.0 copy-start.5
  29.7 0.0 copy-start.13
  29.7 17.4 %shard_map.85 = (bf16[16,2,16,384]{3,2,1,0:T(8,128)(2,1)S(1)}, bf16[2,32,16,384]{3,2,1,0:T(8,128)(2,1)S(1)}) custom-call(bf16[2,16,16,384]{3,2,1,0:T(8,128)(2,1)S(1)} %pad_maximum_fusion.1.x_ref, bf16[2,16,16,384]{3,2,1,0:T(8,128)(2,1)S(1)} %copy-done.1), custom_call_target="tpu_custom_call" | custom-call | tf_op jit(solution)/shard_map/pallas_call | solution.py:147
  47.2 0.0 copy-start.7
  47.2 0.0 copy-done.10
  47.2 0.0 copy-start.3
  47.2 0.6 convolution_bitcast_fusion
  47.8 0.0 copy-done.5
  47.8 0.0 copy-done.13
  47.8 0.0 copy-start.6
  47.8 0.8 fusion.29
  48.6 0.0 copy-done.7
  48.6 0.0 copy-done.3
  48.6 1.3 %convolution_bitcast_fusion.1 = f32[8,196,32]{1,2,0:T(8,128)} fusion(bf16[8,196,384]{2,0,1:T(8,128)(2,1)S(1)} %copy-done.3, bf16[32,8,384]{2,1,0:T(8,128)(2,1)S(1)} %get-tuple-element.17), kind=kOutput, calls=%fused_computation.38 | convolution fusion | flops 38535168 | bytes 1601536 | tf_op jit(solution)/shard_map/bpd,sbd->bps/dot_general | solution.py:282
  49.9 2.7 %convolution_bitcast_fusion.2 = f32[32,384]{1,0:T(8,128)S(1)} fusion(f32[8,196,32]{1,2,0:T(8,128)} %fusion.29, f32[8,196,32]{1,2,0:T(8,128)} %convolution_bitcast_fusion.1, bf16[8,196,384]{2,0,1:T(8,128)(2,1)} %param.5, f32[8,196,32]{1,2,0:T(8,128)S(1)} %copy-done.6, f32[8,32]{1,0:T(8,128)S(1)} %get-tuple-element.14, f32[8,32]{1,0:T(8,128)S(1)} %get-tuple-element.12), kind=kOutput, calls=%fused_computation.44 | convolution fusion | flops 38987204 | bytes 1857536 | tf_op jit(solution)/shard_map/bps,bpd->sd/dot_general | solution.py:293
  52.6 0.7 reshape.52.x_ref
  53.2 15.6 %shard_map.86 = f32[16,2,384]{2,1,0:T(2,128)} custom-call(f32[16,2,384]{2,1,0:T(2,128)} %reshape.52.x_ref), custom_call_target="tpu_custom_call" | custom-call | tf_op jit(solution)/shard_map/pallas_call | solution.py:214
  68.8 1.5 %reshape.53 = f32[32,384]{1,0:T(8,128)} reshape(f32[16,2,384]{2,1,0:T(2,128)} %shard_map.86) | data formatting | bytes 98304 | tf_op jit(solution)/shard_map/reshape | solution.py:232
  70.3 1.7 %fusion.16 = f32[2,256,768]{2,1,0:T(8,128)} fusion(bf16[2,384,1536]{2,1,0:T(8,128)(2,1)S(1)} %copy-done, s32[]{:T(128)S(6)} %select_n.4, bf16[2,32,16,384]{3,2,1,0:T(8,128)(2,1)S(1)} %get-tuple-element.7), kind=kOutput, calls=%fused_computation.23 | convolution fusion | flops 301989888 | bytes 3145732 | tf_op jit(solution)/shard_map/jrd,jdf->jrf/dot_general | solution.py:254
  72.0 2.5 %fusion.89 = f32[8,196,384]{2,1,0:T(8,128)} fusion(bf16[32,8,384]{2,1,0:T(8,128)(2,1)S(1)} %copy-done.8, f32[8,196,32]{1,2,0:T(8,128)S(1)} %copy-done.6, f32[8,32]{1,0:T(8,128)S(1)} %get-tuple-element.14, f32[8,32]{1,0:T(8,128)S(1)} %get-tuple-element.12), kind=kOutput, calls=%fused_computation.94 | convolution fusion | flops 38685696 | bytes 2807808 | tf_op jit(solution)/shard_map/bps,sbd->bpd/dot_general | solution.py:290
  74.4 4.1 %add_convert_fusion = bf16[8,196,384]{2,1,0:T(8,128)(2,1)} fusion(f32[8,196,384]{2,1,0:T(8,128)} %fusion.89, f32[8,196,32]{1,2,0:T(8,128)} %fusion.29, f32[8,196,32]{1,2,0:T(8,128)} %convolution_bitcast_fusion.1, bf16[384,32]{0,1:T(8,128)(2,1)S(1)} %copy-done.11, f32[8,196,32]{1,2,0:T(8,128)S(1)} %copy-done.6, f32[8,32]{1,0:T(8,128)S(1)} %get-tuple-element.14, ...), kind=kOutput, calls=%fused_computation.2 | convolution fusion | flops 40191428 | bytes 4241408 | tf_op jit(solution)/shard_map/bps,ds->bpd/dot_general | solution.py:291
  78.5 2.5 %copy.20 = bf16[8,196,384]{2,0,1:T(8,128)(2,1)} copy(bf16[8,196,384]{2,1,0:T(8,128)(2,1)} %add_convert_fusion) | data formatting | bytes 2408448
  81.0 4.8 %fusion.23 = f32[2,384,768]{2,1,0:T(8,128)} fusion(f32[2,256,768]{2,1,0:T(8,128)} %fusion.16, bf16[2,1536,384]{2,1,0:T(8,128)(2,1)} %param.8, s32[]{:T(128)S(6)} %select_n.4, bf16[2,32,16,384]{3,2,1,0:T(8,128)(2,1)S(1)} %get-tuple-element.7), kind=kOutput, calls=%fused_computation.27 | convolution fusion | flops 611844096 | bytes 5898244 | tf_op jit(solution)/shard_map/jrd,jrf->jdf/dot_general | solution.py:278
  85.8 3.6 %fusion.41 = f32[2,768,384]{2,1,0:T(8,128)} fusion(f32[2,256,768]{2,1,0:T(8,128)} %fusion.16, bf16[2,32,16,384]{3,2,1,0:T(8,128)(2,1)S(1)} %get-tuple-element.7), kind=kOutput, calls=%fused_computation.50 | convolution fusion | flops 305528832 | bytes 4325376 | tf_op jit(solution)/shard_map/jrf,jrd->jfd/dot_general | solution.py:279
  (10 shorter events, 0.1 us)
Async XLA Ops:
  0.6 21.1 %copy-start = (bf16[2,384,1536]{2,1,0:T(8,128)(2,1)S(1)}, bf16[2,384,1536]{2,1,0:T(8,128)(2,1)}, u32[]{:S(2)}) copy-start(bf16[2,384,1536]{2,1,0:T(8,128)(2,1)} %param.7) | copy-start | bytes 7077892
  3.1 2.7 %copy-start.4 = (f32[8,196,32]{1,2,0:T(8,128)}, f32[8,196,32]{1,2,0:T(8,128)S(1)}, u32[]{:S(2)}) copy-start(f32[8,196,32]{1,2,0:T(8,128)S(1)} %copy.22) | copy-start | bytes 602116
  3.1 2.2 %copy-start.2 = (bf16[8,196,384]{2,0,1:T(8,128)(2,1)S(1)}, bf16[8,196,384]{2,0,1:T(8,128)(2,1)}, u32[]{:S(2)}) copy-start(bf16[8,196,384]{2,0,1:T(8,128)(2,1)} %param.5) | copy-start | bytes 3612676
  3.3 2.5 %copy-start.12 = (f32[8,196]{1,0:T(8,128)}, f32[8,196]{1,0:T(8,128)S(1)}, u32[]{:S(2)}) copy-start(f32[8,196]{1,0:T(8,128)S(1)} %get-tuple-element.15) | copy-start | bytes 18820
  21.7 2.8 %copy-start.14 = (bf16[2,1536,384]{2,1,0:T(8,128)(2,1)S(1)}, bf16[2,1536,384]{2,1,0:T(8,128)(2,1)}, u32[]{:S(2)}) copy-start(bf16[2,1536,384]{2,1,0:T(8,128)(2,1)} %param.8) | copy-start | bytes 7077892
  23.4 1.1 %copy-start.9 = (f32[2,128,1536]{2,1,0:T(8,128)}, f32[2,128,1536]{2,1,0:T(8,128)S(1)}, u32[]{:S(2)}) copy-start(f32[2,128,1536]{2,1,0:T(8,128)S(1)} %fusion.83) | copy-start | bytes 4718596
  24.5 1.0 %copy-start.1 = (bf16[2,16,16,384]{3,2,1,0:T(8,128)(2,1)S(1)}, bf16[2,16,16,384]{3,2,1,0:T(8,128)(2,1)}, u32[]{:S(2)}) copy-start(bf16[2,16,16,384]{3,2,1,0:T(8,128)(2,1)} %shard_map.84.here_ref) | copy-start | bytes 1179652
  29.6 17.6 %copy-start.10 = (bf16[8,196,384]{2,0,1:T(8,128)(2,1)S(1)}, bf16[8,196,384]{2,0,1:T(8,128)(2,1)}, u32[]{:S(2)}) copy-start(bf16[8,196,384]{2,0,1:T(8,128)(2,1)} %param.9) | copy-start | bytes 3612676
  29.7 18.1 %copy-start.5 = (f32[8,196,32]{1,2,0:T(8,128)S(1)}, f32[8,196,32]{1,2,0:T(8,128)}, u32[]{:S(2)}) copy-start(f32[8,196,32]{1,2,0:T(8,128)} %copy-done.4) | copy-start | bytes 602116
  29.7 18.1 %copy-start.13 = (f32[8,196]{1,0:T(8,128)S(1)}, f32[8,196]{1,0:T(8,128)}, u32[]{:S(2)}) copy-start(f32[8,196]{1,0:T(8,128)} %copy-done.12) | copy-start | bytes 18820
  47.2 1.5 %copy-start.7 = (bf16[32,8,384]{2,1,0:T(8,128)(2,1)}, bf16[32,8,384]{2,1,0:T(8,128)(2,1)S(1)}, u32[]{:S(2)}) copy-start(bf16[32,8,384]{2,1,0:T(8,128)(2,1)S(1)} %get-tuple-element.17) | copy-start | bytes 589828
  47.2 1.5 %copy-start.3 = (bf16[8,196,384]{2,0,1:T(8,128)(2,1)S(1)}, bf16[8,196,384]{2,0,1:T(8,128)(2,1)}, u32[]{:S(2)}) copy-start(bf16[8,196,384]{2,0,1:T(8,128)(2,1)} %param.5) | copy-start | bytes 3612676
  47.8 2.1 %copy-start.6 = (f32[8,196,32]{1,2,0:T(8,128)S(1)}, f32[8,196,32]{1,2,0:T(8,128)}, u32[]{:S(2)}) copy-start(f32[8,196,32]{1,2,0:T(8,128)} %copy-done.4) | copy-start | bytes 602116
  70.3 1.7 %copy-start.8 = (bf16[32,8,384]{2,1,0:T(8,128)(2,1)S(1)}, bf16[32,8,384]{2,1,0:T(8,128)(2,1)}, u32[]{:S(2)}) copy-start(bf16[32,8,384]{2,1,0:T(8,128)(2,1)} %copy-done.7) | copy-start | bytes 589828
  72.0 2.5 %copy-start.11 = (bf16[384,32]{0,1:T(8,128)(2,1)S(1)}, bf16[384,32]{0,1:T(8,128)(2,1)}, u32[]{:S(2)}) copy-start(bf16[384,32]{0,1:T(8,128)(2,1)} %param.6) | copy-start | bytes 73732
